TPU v7x, 256 devices: a whole 4x4x8 slice. The times are simulated.
256 devices in a mesh: blk: 64 (over y_lo, z, x), row: 4 (over y_hi, core).
Axes of the slice: x: 4, y: 4 (y_hi: 2, y_lo: 2; y = y_hi * 2 + y_lo), z: 8, core: 2. Of those that a mesh axis runs over, the one named last changes fastest.
Arguments:
- transmission: float32 [16384, 2, 8192], P(('blk', 'row')), may hold values from -64 to 64, as said below
- assignment: int32 [256], replicated, may hold values from 0 to 255, each once
- pairing: int32 [2, 64], replicated, may hold values from 0 to 2
Outputs:
- rotated: float32 [16384, 2, 8192], P(('blk', 'row'))
Inputs may be any that keep to these rules, and one draw needn't show every extreme that they name: `transmission`: entries are real and imaginary parts of a measured speckle field; columns and rows have differing gains. `assignment`: A permutation of the block numbers.
All inputs are finite; a program needn't handle non-finite values.
Results may differ from a plain program's by a relative error of at most 0.00016.
Values sent between devices are 32-bit elements; how exact they have to be, the bound alone decides.
A program may use at most 128 MiB of HBM per device.

v0:
```python
import jax
import jax.numpy as jnp
from jax import lax
from jax.sharding import PartitionSpec as P

ROWS = 16384
BLOCK = 32
SLOTS = 4
ROUNDS = 2
NS_STEPS = 6


def shifted(block, axis, distance):
    devices = range(lax.axis_size(axis))
    route = [((i - distance) % len(devices), i) for i in devices]
    return lax.ppermute(block, axis, route)


def kernel_rotation(real_part, imag_part):
    kernel = jnp.concatenate(
        [
            jnp.concatenate([real_part, imag_part], axis=1),
            jnp.concatenate([-imag_part, real_part], axis=1),
        ],
        axis=0,
    )
    scale = jnp.sqrt(jnp.sum(kernel * kernel))
    eye = jnp.eye(kernel.shape[0], dtype=jnp.float32)
    upper = kernel / scale
    lower = eye
    for step in range(NS_STEPS):
        middle = 1.5 * eye - 0.5 * jnp.dot(lower, upper, precision=lax.Precision.HIGHEST)
        upper = jnp.dot(upper, middle, precision=lax.Precision.HIGHEST)
        lower = jnp.dot(middle, lower, precision=lax.Precision.HIGHEST)
    return lower * jnp.sqrt(ROWS / scale)


def pair_rotation(gram):
    half = gram.shape[0] // 2
    real_part = gram[:half, :half] + gram[half:, half:]
    imag_part = gram[:half, half:] - gram[half:, :half]
    return kernel_rotation(real_part, imag_part)


def local_gram(joined):
    return jnp.dot(joined.T, joined, precision=lax.Precision.HIGHEST)


def summed_pair(joined):
    gram = lax.psum(local_gram(joined), "row")
    return jnp.dot(joined, pair_rotation(gram), precision=lax.Precision.HIGHEST)


def column_index(held, total_cols):
    parts = jnp.arange(2, dtype=jnp.int32)[None, :, None, None] * total_cols
    starts = held[:, None, :, None] * BLOCK
    within = jnp.arange(BLOCK, dtype=jnp.int32)[None, None, None, :]
    return (parts + starts + within).reshape(-1)


def slot_columns(slots):
    parts = jnp.arange(2, dtype=jnp.int32)[:, None, None] * (SLOTS * BLOCK)
    starts = slots[None, :, None] * BLOCK
    within = jnp.arange(BLOCK, dtype=jnp.int32)[None, None, :]
    return (parts + starts + within).reshape(-1)


def inverse_of(index):
    return (
        jnp.zeros(index.shape, jnp.int32).at[index].set(jnp.arange(index.shape[0], dtype=jnp.int32))
    )


def turn_held(held):
    return jnp.stack(
        [held[:, 0], jnp.roll(held[:, 1], 1), jnp.roll(held[:, 2], -1), held[:, 3]], axis=1
    )


def on_device(transmission, assignment, pairing):
    nblk = lax.axis_size("blk")
    me_blk = lax.axis_index("blk")
    row_part = transmission.shape[0]
    total_cols = transmission.shape[2]
    orders = jnp.array([[0, 1, 2, 3], [0, 2, 1, 3], [0, 3, 1, 2]], dtype=jnp.int32)
    held = assignment.reshape(nblk, SLOTS)
    flat = transmission.reshape(row_part, 2 * total_cols)
    outgoing = jnp.take(flat, column_index(held, total_cols), axis=1)
    blocks = lax.all_to_all(outgoing, "blk", split_axis=1, concat_axis=0, tiled=True)
    owned_rows = blocks.shape[0]
    for rnd in range(ROUNDS):
        pick = pairing[rnd, me_blk]
        order = orders[pick]
        first_cols = slot_columns(order[0:2])
        second_cols = slot_columns(order[2:4])
        first = jnp.take(blocks, first_cols, axis=1)
        second = jnp.take(blocks, second_cols, axis=1)
        new_first = summed_pair(first)
        new_second = summed_pair(second)
        joined = jnp.concatenate([new_first, new_second], axis=1)
        back = inverse_of(jnp.concatenate([first_cols, second_cols]))
        blocks = jnp.take(joined, back, axis=1)
        if rnd < ROUNDS - 1:
            lanes = owned_rows * 2 * BLOCK // 128
            up_cols = slot_columns(jnp.array([1], dtype=jnp.int32))
            down_cols = slot_columns(jnp.array([2], dtype=jnp.int32))
            moved_up = shifted(jnp.take(blocks, up_cols, axis=1).reshape(lanes, 128), "blk", 1)
            moved_down = shifted(jnp.take(blocks, down_cols, axis=1).reshape(lanes, 128), "blk", -1)
            blocks = blocks.at[:, up_cols].set(moved_up.reshape(owned_rows, 2 * BLOCK))
            blocks = blocks.at[:, down_cols].set(moved_down.reshape(owned_rows, 2 * BLOCK))
            held = turn_held(held)
    returned = lax.all_to_all(blocks, "blk", split_axis=0, concat_axis=1, tiled=True)
    placed = column_index(held, total_cols)
    rotated = jnp.take(returned, inverse_of(placed), axis=1)
    return rotated.reshape(row_part, 2, total_cols)


def solution(mesh):
    placed = (P(("blk", "row"), None, None), P(), P())
    return jax.shard_map(
        on_device,
        mesh=mesh,
        in_specs=placed,
        out_specs=P(("blk", "row"), None, None),
        check_vma=False,
    )
```

profile of v0, /device:TPU:6, one launch (start us, length us, event | category | flops | bytes accessed | tf_op | source)
XLA Modules:
  0.0 666.9 jit_solution(6179644993815325899)
XLA Ops:
  10.4 8.4 %copy.43 = f32[64,2,8192]{0,2,1:T(8,128)} copy(f32[64,2,8192]{2,1,0:T(2,128)} %param.14) | data formatting | bytes 8388608 | tf_op args[0]
  18.8 58.2 %gather_fusion = f32[16384,64]{1,0:T(8,128)} fusion(f32[64,16384]{0,1:T(8,128)} %bitcast.203, s32[16384]{0:T(1024)S(1)} %fusion.68), kind=kCustom, calls=%fused_computation.clone | custom fusion | bytes 8454144 | tf_op jit(solution)/shard_map/jit(_take)/gather | solution.py:88
  77.0 13.1 %broadcast_select_fusion.1 = f32[16384,64]{1,0:T(8,128)} fusion(f32[16384,64]{1,0:T(8,128)} %gather_fusion, pred[16384]{0:T(1024)(128)(4,1)S(1)} %compare_and_fusion.1), kind=kLoop, calls=%fused_computation.20 | loop fusion | flops 1048576 | bytes 8404992 | tf_op jit(solution)/shard_map/jit(_take)/select_n | solution.py:88
  90.1 6.8 %copy.44 = f32[64,64,256]{2,0,1:T(8,128)} copy(f32[64,64,256]{0,2,1:T(8,128)} %bitcast.204) | data formatting | bytes 8388608 | tf_op jit(solution)/shard_map/all_to_all | solution.py:89
  96.9 13.3 %all-to-all-start = ((f32[64,64,256]{2,0,1:T(8,128)}), f32[64,64,256]{2,0,1:T(8,128)}, u32[]{:S(2)}, u32[]{:S(2)}) async-start(f32[64,64,256]{2,0,1:T(8,128)} %copy.44), calls=%async_computation | async-start | bytes 8388608 | tf_op jit(solution)/shard_map/all_to_all | solution.py:89
  117.8 87.9 %all-to-all-done = f32[64,64,256]{2,0,1:T(8,128)} async-done(((f32[64,64,256]{2,0,1:T(8,128)}), f32[64,64,256]{2,0,1:T(8,128)}, u32[]{:S(2)}, u32[]{:S(2)}) %all-to-all-start) | async-done | bytes 4194336 | tf_op jit(solution)/shard_map/all_to_all | solution.py:89
  205.7 5.6 copy.45
  211.3 5.6 gather_fusion.2
  216.9 4.4 gather_fusion.1
  221.3 4.9 fusion.10
  231.0 40.0 %all-reduce.7.cloned.1.call-done = (f32[128,128]{1,0:T(8,128)}, f32[128,128]{1,0:T(8,128)}) async-done(((f32[128,128]{1,0:T(8,128)}, f32[128,128]{1,0:T(8,128)}), (f32[128,128]{1,0:T(8,128)}, f32[128,128]{1,0:T(8,128)})) %all-reduce.7.cloned.1.call-update) | async-done | bytes 131088 | tf_op jit(solution)/shard_map/psum | solution.py:50
  281.9 5.1 fusion.8
  292.1 7.8 %gather_fusion.3 = f32[256,4096]{1,0:T(8,128)} fusion(f32[4096,256]{0,1:T(8,128)} %pad_maximum_fusion, s32[1024]{0:T(1024)S(1)} %pad_clamp_fusion.5), kind=kCustom, calls=%fused_computation.2.clone | custom fusion | bytes 8389632 | tf_op jit(solution)/shard_map/jit(_take)/gather | solution.py:102
  299.9 5.2 select_bitcast_fusion.1
  320.7 21.5 %collective-permute-done = f32[2048,128]{1,0:T(8,128)} collective-permute-done((f32[2048,128]{1,0:T(8,128)}, f32[2048,128]{1,0:T(8,128)}, u32[]{:S(2)}, u32[]{:S(2)}) %collective-permute-start) | collective-permute-done | bytes 1048608 | tf_op jit(solution)/shard_map/ppermute | solution.py:16
  352.6 5.3 scatter_fusion
  357.9 5.5 scatter_fusion.1
  363.4 5.6 gather_fusion.7
  369.0 4.4 gather_fusion.6
  373.5 4.9 fusion.2
  381.1 44.9 %all-reduce.5.cloned.1.call-done = (f32[128,128]{1,0:T(8,128)}, f32[128,128]{1,0:T(8,128)}) async-done(((f32[128,128]{1,0:T(8,128)}, f32[128,128]{1,0:T(8,128)}), (f32[128,128]{1,0:T(8,128)}, f32[128,128]{1,0:T(8,128)})) %all-reduce.5.cloned.1.call-update) | async-done | bytes 131088 | tf_op jit(solution)/shard_map/psum | solution.py:50
  436.8 5.3 fusion
  447.3 7.8 %gather_fusion.8 = f32[256,4096]{1,0:T(8,128)} fusion(f32[4096,256]{0,1:T(8,128)} %pad_maximum_fusion.1, s32[1024]{0:T(1024)S(1)} %pad_clamp_fusion), kind=kCustom, calls=%fused_computation.8.clone | custom fusion | bytes 8389632 | tf_op jit(solution)/shard_map/jit(_take)/gather | solution.py:102
  455.1 4.8 select_bitcast_fusion
  459.9 5.6 copy.51
  465.5 10.7 %all-to-all-start.1 = ((f32[64,64,256]{2,1,0:T(8,128)}), f32[64,64,256]{2,1,0:T(8,128)}, u32[]{:S(2)}, u32[]{:S(2)}) async-start(f32[64,64,256]{2,1,0:T(8,128)} %bitcast.206), calls=%async_computation.1 | async-start | bytes 8388608 | tf_op jit(solution)/shard_map/all_to_all | solution.py:112
  476.8 60.3 %scatter_custom_fusion.4 = s32[16384]{0:T(1024)S(1)} fusion(s32[16384]{0:T(1024)S(1)} %bitcast.209, s32[16384]{0:T(1024)S(1)} %iota.215, s32[]{:T(128)} %constant.15.clone.1), kind=kCustom, calls=%fused_computation.148 | custom fusion | bytes 65540 | tf_op jit(solution)/shard_map/scatter | solution.py:70
  537.2 35.8 %all-to-all-done.1 = f32[64,64,256]{2,1,0:T(8,128)} async-done(((f32[64,64,256]{2,1,0:T(8,128)}), f32[64,64,256]{2,1,0:T(8,128)}, u32[]{:S(2)}, u32[]{:S(2)}) %all-to-all-start.1) | async-done | bytes 4194336 | tf_op jit(solution)/shard_map/all_to_all | solution.py:112
  573.0 6.9 %copy.52 = f32[64,64,256]{0,2,1:T(8,128)} copy(f32[64,64,256]{2,0,1:T(8,128)} %bitcast.32) | data formatting | bytes 8388608 | tf_op jit(solution)/shard_map/all_to_all | solution.py:112
  579.9 58.2 %gather_fusion.9 = f32[16384,64]{1,0:T(8,128)} fusion(f32[64,16384]{0,1:T(8,128)} %bitcast.202, s32[16384]{0:T(1024)S(1)} %fusion.69), kind=kCustom, calls=%fused_computation.4.clone | custom fusion | bytes 8454144 | tf_op jit(solution)/shard_map/jit(_take)/gather | solution.py:114
  638.1 13.1 %broadcast_select_fusion = f32[16384,64]{1,0:T(8,128)} fusion(f32[16384,64]{1,0:T(8,128)} %gather_fusion.9, pred[16384]{0:T(1024)(128)(4,1)S(1)} %compare_and_fusion), kind=kLoop, calls=%fused_computation.19 | loop fusion | flops 1048576 | bytes 8404992 | tf_op jit(solution)/shard_map/jit(_take)/select_n | solution.py:114
  651.2 8.6 %copy.53 = f32[64,2,8192]{2,1,0:T(2,128)} copy(f32[64,2,8192]{0,2,1:T(8,128)} %bitcast.205) | data formatting | bytes 8388608 | tf_op jit(solution)/shard_map/reshape | solution.py:115
  (191 shorter events, 69.7 us)
Async XLA Ops:
  96.9 13.4 %copy-start.4 = (s32[2,64]{1,0:T(2,128)S(1)}, s32[2,64]{1,0:T(2,128)}, u32[]{:S(2)}) copy-start(s32[2,64]{1,0:T(2,128)} %param.16) | copy-start | bytes 1540
  96.9 17.8 %copy-start.5 = (s32[3,4]{1,0:T(4,128)S(1)}, s32[3,4]{1,0:T(4,128)}, u32[]{:S(2)}) copy-start(s32[3,4]{1,0:T(4,128)} %constant.22.clone) | copy-start | bytes 148
  96.9 108.8 %all-to-all-start = ((f32[64,64,256]{2,0,1:T(8,128)}), f32[64,64,256]{2,0,1:T(8,128)}, u32[]{:S(2)}, u32[]{:S(2)}) async-start(f32[64,64,256]{2,0,1:T(8,128)} %copy.44), calls=%async_computation | async-start | bytes 8388608 | tf_op jit(solution)/shard_map/all_to_all | solution.py:89
  110.2 160.8 %all-reduce.7.cloned.1.call-start = ((), (), s32[]{:S(2)}) async-start(), calls=%async_computation.3 | async-start | bytes 262144 | tf_op jit(solution)/shard_map/psum | solution.py:50
  228.9 197.0 %all-reduce.5.cloned.1.call-start = ((), (), s32[]{:S(2)}) async-start(), calls=%async_computation.2 | async-start | bytes 262144 | tf_op jit(solution)/shard_map/psum | solution.py:50
  271.0 5.6 copy-start.2
  287.4 2.2 copy-start
  316.6 25.7 %collective-permute-start = (f32[2048,128]{1,0:T(8,128)}, f32[2048,128]{1,0:T(8,128)}, u32[]{:S(2)}, u32[]{:S(2)}) collective-permute-start(f32[2048,128]{1,0:T(8,128)} %reshape.609), channel_id=1, source_target_pairs={{252,0},{0,4},{4,8},{8,12},{12,16},{16,20},{20,24},{24,28},{28,32}... | collective-permute-start | bytes 3145736 | tf_op jit(solution)/shard_map/ppermute | solution.py:16
  320.2 27.5 %collective-permute-start.1 = (f32[2048,128]{1,0:T(8,128)}, f32[2048,128]{1,0:T(8,128)}, u32[]{:S(2)}, u32[]{:S(2)}) collective-permute-start(f32[2048,128]{1,0:T(8,128)} %reshape.611), channel_id=1, source_target_pairs={{4,0},{8,4},{12,8},{16,12},{20,16},{24,20},{28,24},{32,28},{36,32}... | collective-permute-start | bytes 3145736 | tf_op jit(solution)/shard_map/ppermute | solution.py:16
  425.9 5.6 copy-start.3
  442.6 2.2 copy-start.1
  465.5 107.5 %all-to-all-start.1 = ((f32[64,64,256]{2,1,0:T(8,128)}), f32[64,64,256]{2,1,0:T(8,128)}, u32[]{:S(2)}, u32[]{:S(2)}) async-start(f32[64,64,256]{2,1,0:T(8,128)} %bitcast.206), calls=%async_computation.1 | async-start | bytes 8388608 | tf_op jit(solution)/shard_map/all_to_all | solution.py:112
Sparse Core Ops, SparseCore 0:
  229.0 41.9 all-reduce.6
  381.2 44.7 all-reduce.4
where the time goes:
time: 673 us; the launch traced here: 667 us
  local copies, waits for them, and re-layouts  292 us (43%)
  waiting for transfers between devices  233 us (35%)
  other arithmetic  49.8 us (7%)
  matrix products  44.1 us (7%)
  starting transfers between devices  26.1 us (4%)
  between operations  21.6 us (3%)
    all_to_all x1, waiting for transfers between devices, on_device(): lax.all_to_all(outgoing, 'blk', split_axis=1, concat_axis=0, tiled=True)  87.9 us
    psum x2, waiting for transfers between devices, summed_pair(): gram = lax.psum(local_gram(joined), 'row')  84.8 us
    scatter x3, local copies, waits for them, and re-layouts, inverse_of(): jnp.zeros(index.shape, jnp.int32).at[index]  63.5 us
    gather x1, local copies, waits for them, and re-layouts, on_device(): outgoing = jnp.take(flat, column_index(held, total_cols), axis=1)  58.2 us
    gather x1, local copies, waits for them, and re-layouts, on_device(): rotated = jnp.take(returned, inverse_of(placed), axis=1)  58.2 us
    all_to_all x1, waiting for transfers between devices, on_device(): lax.all_to_all(blocks, 'blk', split_axis=0, concat_axis=1, tiled=True)  35.8 us
    ppermute x2, waiting for transfers between devices, shifted(): return lax.ppermute(block, axis, route)  24.8 us
    gather x2, local copies, waits for them, and re-layouts, on_device(): blocks = jnp.take(joined, back, axis=1)  15.6 us
  transfers between devices with their start and end apart: 6, of which 6 were waited for; matrix products, arithmetic and copies ran while one was open for 11% of the time, Pallas kernels for 0%

commit v1 on v0

--- a/solution.py
+++ b/solution.py
@@ -47,7 +47,7 @@
 
 
 def summed_pair(joined):
-    gram = lax.psum(local_gram(joined), "row")
+    gram = jnp.sum(lax.all_gather(local_gram(joined), "row"), axis=0)
     return jnp.dot(joined, pair_rotation(gram), precision=lax.Precision.HIGHEST)
 
 

time: 673 us -> 610 us (0.906)
  waiting for transfers between devices: 233 us -> 146 us
  blocking collectives: 0 us -> 30.1 us
  between operations: 21.6 us -> 8.42 us
  local copies, waits for them, and re-layouts: 292 us -> 302 us
    psum x2 -> x0, waiting for transfers between devices: 84.8 us -> none  [summed_pair(): gram = lax.psum(local_gram(joined), 'row')]
    all_gather x0 -> x4, blocking collectives: none -> 30.1 us  [summed_pair(): gram = jnp.sum(lax.all_gather(local_gram(joined), 'row'), axis=0)]
    gather x1, local copies, waits for them, and re-layouts: 3.57 us -> 15.4 us  [on_device(): jnp.take(blocks, up_cols, axis=1).reshape(lanes, 128)]
  transfers between devices with their start and end apart: 6 -> 4, of which waited for: 6 -> 4; matrix products, arithmetic and copies ran while one was open for 11% -> 12% of each run, Pallas kernels for 0% -> 0%
where the time goes in v1:
time: 610 us; the launch traced here: 602 us
  local copies, waits for them, and re-layouts  302 us (50%)
  waiting for transfers between devices  146 us (24%)
  other arithmetic  48.1 us (8%)
  matrix products  41.6 us (7%)
  blocking collectives  30.1 us (5%)
  starting transfers between devices  25.6 us (4%)
  between operations  8.42 us (1%)
    all_to_all x1, waiting for transfers between devices, on_device(): lax.all_to_all(outgoing, 'blk', split_axis=1, concat_axis=0, tiled=True)  88 us
    scatter x3, local copies, waits for them, and re-layouts, inverse_of(): jnp.zeros(index.shape, jnp.int32).at[index]  63.1 us
    gather x1, local copies, waits for them, and re-layouts, on_device(): outgoing = jnp.take(flat, column_index(held, total_cols), axis=1)  57.8 us
    gather x1, local copies, waits for them, and re-layouts, on_device(): rotated = jnp.take(returned, inverse_of(placed), axis=1)  57.8 us
    all_to_all x1, waiting for transfers between devices, on_device(): lax.all_to_all(blocks, 'blk', split_axis=0, concat_axis=1, tiled=True)  35.6 us
    all_gather x4, blocking collectives, summed_pair(): gram = jnp.sum(lax.all_gather(local_gram(joined), 'row'), axis=0)  30.1 us
    ppermute x2, waiting for transfers between devices, shifted(): return lax.ppermute(block, axis, route)  21.9 us
    gather x2, local copies, waits for them, and re-layouts, on_device(): blocks = jnp.take(joined, back, axis=1)  15.6 us
  transfers between devices with their start and end apart: 4, of which 4 were waited for; matrix products, arithmetic and copies ran while one was open for 12% of the time, Pallas kernels for 0%

profile of v1, /device:TPU:6, one launch (start us, length us, event | category | flops | bytes accessed | tf_op | source)
XLA Modules:
  0.0 601.5 jit_solution(1130503070791111704)
XLA Ops:
  4.0 8.3 %copy.58 = f32[64,2,8192]{0,2,1:T(8,128)} copy(f32[64,2,8192]{2,1,0:T(2,128)} %param.14) | data formatting | bytes 8388608 | tf_op args[0]
  12.3 57.8 %gather_fusion = f32[16384,64]{1,0:T(8,128)} fusion(f32[64,16384]{0,1:T(8,128)} %bitcast.207, s32[16384]{0:T(1024)S(1)} %fusion.68), kind=kCustom, calls=%fused_computation.clone | custom fusion | bytes 8454144 | tf_op jit(solution)/shard_map/jit(_take)/gather | solution.py:88
  70.0 13.1 %broadcast_select_fusion.1 = f32[16384,64]{1,0:T(8,128)} fusion(f32[16384,64]{1,0:T(8,128)} %gather_fusion, pred[16384]{0:T(1024)(128)(4,1)S(1)} %compare_and_fusion.1), kind=kLoop, calls=%fused_computation.20 | loop fusion | flops 1048576 | bytes 8404992 | tf_op jit(solution)/shard_map/jit(_take)/select_n | solution.py:88
  83.2 6.8 %copy.59 = f32[64,64,256]{2,0,1:T(8,128)} copy(f32[64,64,256]{0,2,1:T(8,128)} %bitcast.208) | data formatting | bytes 8388608 | tf_op jit(solution)/shard_map/all_to_all | solution.py:89
  89.9 13.3 %all-to-all-start = ((f32[64,64,256]{2,0,1:T(8,128)}), f32[64,64,256]{2,0,1:T(8,128)}, u32[]{:S(2)}, u32[]{:S(2)}) async-start(f32[64,64,256]{2,0,1:T(8,128)} %copy.59), calls=%async_computation | async-start | bytes 8388608 | tf_op jit(solution)/shard_map/all_to_all | solution.py:89
  110.8 88.0 %all-to-all-done = f32[64,64,256]{2,0,1:T(8,128)} async-done(((f32[64,64,256]{2,0,1:T(8,128)}), f32[64,64,256]{2,0,1:T(8,128)}, u32[]{:S(2)}, u32[]{:S(2)}) %all-to-all-start) | async-done | bytes 4194336 | tf_op jit(solution)/shard_map/all_to_all | solution.py:89
  198.7 5.6 copy.60
  204.3 4.4 gather_fusion.2
  210.8 7.5 %all-gather.1 = f32[512,128]{1,0:T(8,128)S(1)} all-gather(f32[128,128]{1,0:T(8,128)S(1)} %fusion.10), channel_id=3, replica_groups=mesh['blk'=64,'row'=4] {'row'}, dimensions={0}, use_global_device_ids=true | all-gather | bytes 327680 | tf_op jit(solution)/shard_map/all_gather | solution.py:50
  223.2 5.7 gather_fusion.1
  228.9 4.3 fusion.14
  233.1 7.7 %all-gather = f32[512,128]{1,0:T(8,128)S(1)} all-gather(f32[128,128]{1,0:T(8,128)S(1)} %fusion.14), channel_id=2, replica_groups=mesh['blk'=64,'row'=4] {'row'}, dimensions={0}, use_global_device_ids=true | all-gather | bytes 327680 | tf_op jit(solution)/shard_map/all_gather | solution.py:50
  256.5 7.8 %gather_fusion.3 = f32[256,4096]{1,0:T(8,128)} fusion(f32[4096,256]{0,1:T(8,128)} %pad_maximum_fusion, s32[1024]{0:T(1024)S(1)} %pad_clamp_fusion.5), kind=kCustom, calls=%fused_computation.2.clone | custom fusion | bytes 8389632 | tf_op jit(solution)/shard_map/jit(_take)/gather | solution.py:102
  264.3 4.8 select_bitcast_fusion.1
  272.7 15.4 %gather_fusion.4 = f32[64,4096]{1,0:T(8,128)S(1)} fusion(f32[4096,256]{0,1:T(8,128)} %select_bitcast_fusion.1, s32[1024]{0:T(1024)S(1)} %get-tuple-element.62), kind=kCustom, calls=%fused_computation.3.clone | custom fusion | bytes 2097408 | tf_op jit(solution)/shard_map/jit(_take)/gather | solution.py:107
  298.2 19.9 %collective-permute-done = f32[2048,128]{1,0:T(8,128)} collective-permute-done((f32[2048,128]{1,0:T(8,128)}, f32[2048,128]{1,0:T(8,128)}, u32[]{:S(2)}, u32[]{:S(2)}) %collective-permute-start) | collective-permute-done | bytes 1048608 | tf_op jit(solution)/shard_map/ppermute | solution.py:16
  327.2 5.3 scatter_fusion
  332.5 5.3 scatter_fusion.1
  337.8 4.4 gather_fusion.7
  344.3 7.3 %all-gather.3 = f32[512,128]{1,0:T(8,128)S(1)} all-gather(f32[128,128]{1,0:T(8,128)S(1)} %fusion.2), channel_id=5, replica_groups=mesh['blk'=64,'row'=4] {'row'}, dimensions={0}, use_global_device_ids=true | all-gather | bytes 327680 | tf_op jit(solution)/shard_map/all_gather | solution.py:50
  356.5 5.7 gather_fusion.6
  366.5 7.6 %all-gather.2 = f32[512,128]{1,0:T(8,128)S(1)} all-gather(f32[128,128]{1,0:T(8,128)S(1)} %fusion.6), channel_id=4, replica_groups=mesh['blk'=64,'row'=4] {'row'}, dimensions={0}, use_global_device_ids=true | all-gather | bytes 327680 | tf_op jit(solution)/shard_map/all_gather | solution.py:50
  389.7 7.8 %gather_fusion.8 = f32[256,4096]{1,0:T(8,128)} fusion(f32[4096,256]{0,1:T(8,128)} %pad_maximum_fusion.1, s32[1024]{0:T(1024)S(1)} %pad_clamp_fusion), kind=kCustom, calls=%fused_computation.8.clone | custom fusion | bytes 8389632 | tf_op jit(solution)/shard_map/jit(_take)/gather | solution.py:102
  397.5 4.8 select_bitcast_fusion
  402.3 5.6 copy.66
  407.9 10.3 %all-to-all-start.1 = ((f32[64,64,256]{2,1,0:T(8,128)}), f32[64,64,256]{2,1,0:T(8,128)}, u32[]{:S(2)}, u32[]{:S(2)}) async-start(f32[64,64,256]{2,1,0:T(8,128)} %bitcast.210), calls=%async_computation.1 | async-start | bytes 8388608 | tf_op jit(solution)/shard_map/all_to_all | solution.py:112
  418.7 60.3 %scatter_custom_fusion.4 = s32[16384]{0:T(1024)S(1)} fusion(s32[16384]{0:T(1024)S(1)} %bitcast.217, s32[16384]{0:T(1024)S(1)} %iota.215, s32[]{:T(128)} %constant.15.clone.1), kind=kCustom, calls=%fused_computation.148 | custom fusion | bytes 65540 | tf_op jit(solution)/shard_map/scatter | solution.py:70
  479.1 35.6 %all-to-all-done.1 = f32[64,64,256]{2,1,0:T(8,128)} async-done(((f32[64,64,256]{2,1,0:T(8,128)}), f32[64,64,256]{2,1,0:T(8,128)}, u32[]{:S(2)}, u32[]{:S(2)}) %all-to-all-start.1) | async-done | bytes 4194336 | tf_op jit(solution)/shard_map/all_to_all | solution.py:112
  514.7 6.9 %copy.67 = f32[64,64,256]{0,2,1:T(8,128)} copy(f32[64,64,256]{2,0,1:T(8,128)} %bitcast.36) | data formatting | bytes 8388608 | tf_op jit(solution)/shard_map/all_to_all | solution.py:112
  521.6 57.8 %gather_fusion.9 = f32[16384,64]{1,0:T(8,128)} fusion(f32[64,16384]{0,1:T(8,128)} %bitcast.206, s32[16384]{0:T(1024)S(1)} %fusion.69), kind=kCustom, calls=%fused_computation.4.clone | custom fusion | bytes 8454144 | tf_op jit(solution)/shard_map/jit(_take)/gather | solution.py:114
  579.4 13.1 %broadcast_select_fusion = f32[16384,64]{1,0:T(8,128)} fusion(f32[16384,64]{1,0:T(8,128)} %gather_fusion.9, pred[16384]{0:T(1024)(128)(4,1)S(1)} %compare_and_fusion), kind=kLoop, calls=%fused_computation.19 | loop fusion | flops 1048576 | bytes 8404992 | tf_op jit(solution)/shard_map/jit(_take)/select_n | solution.py:114
  592.5 8.6 %copy.68 = f32[64,2,8192]{2,1,0:T(2,128)} copy(f32[64,2,8192]{0,2,1:T(8,128)} %bitcast.209) | data formatting | bytes 8388608 | tf_op jit(solution)/shard_map/reshape | solution.py:115
  (189 shorter events, 76.5 us)
Async XLA Ops:
  89.9 13.3 %copy-start.2 = (s32[2,64]{1,0:T(2,128)S(1)}, s32[2,64]{1,0:T(2,128)}, u32[]{:S(2)}) copy-start(s32[2,64]{1,0:T(2,128)} %param.16) | copy-start | bytes 1540
  89.9 17.6 %copy-start.3 = (s32[3,4]{1,0:T(4,128)S(1)}, s32[3,4]{1,0:T(4,128)}, u32[]{:S(2)}) copy-start(s32[3,4]{1,0:T(4,128)} %constant.22.clone) | copy-start | bytes 148
  89.9 108.8 %all-to-all-start = ((f32[64,64,256]{2,0,1:T(8,128)}), f32[64,64,256]{2,0,1:T(8,128)}, u32[]{:S(2)}, u32[]{:S(2)}) async-start(f32[64,64,256]{2,0,1:T(8,128)} %copy.59), calls=%async_computation | async-start | bytes 8388608 | tf_op jit(solution)/shard_map/all_to_all | solution.py:89
  250.1 3.9 copy-start
  292.4 25.7 %collective-permute-start = (f32[2048,128]{1,0:T(8,128)}, f32[2048,128]{1,0:T(8,128)}, u32[]{:S(2)}, u32[]{:S(2)}) collective-permute-start(f32[2048,128]{1,0:T(8,128)} %reshape.609), channel_id=1, source_target_pairs={{252,0},{0,4},{4,8},{8,12},{12,16},{16,20},{20,24},{24,28},{28,32}... | collective-permute-start | bytes 3145736 | tf_op jit(solution)/shard_map/ppermute | solution.py:16
  294.5 27.8 %collective-permute-start.1 = (f32[2048,128]{1,0:T(8,128)}, f32[2048,128]{1,0:T(8,128)}, u32[]{:S(2)}, u32[]{:S(2)}) collective-permute-start(f32[2048,128]{1,0:T(8,128)} %reshape.611), channel_id=1, source_target_pairs={{4,0},{8,4},{12,8},{16,12},{20,16},{24,20},{28,24},{32,28},{36,32}... | collective-permute-start | bytes 3145736 | tf_op jit(solution)/shard_map/ppermute | solution.py:16
  383.3 3.9 copy-start.1
  407.9 106.9 %all-to-all-start.1 = ((f32[64,64,256]{2,1,0:T(8,128)}), f32[64,64,256]{2,1,0:T(8,128)}, u32[]{:S(2)}, u32[]{:S(2)}) async-start(f32[64,64,256]{2,1,0:T(8,128)} %bitcast.210), calls=%async_computation.1 | async-start | bytes 8388608 | tf_op jit(solution)/shard_map/all_to_all | solution.py:112
